TPU v7x, 256 devices: a whole 4x4x8 slice. The times are simulated.
256 devices in a mesh: cand: 32 (over z, x_hi, core), query: 8 (over y, x_lo).
Axes of the slice: x: 4 (x_hi: 2, x_lo: 2; x = x_hi * 2 + x_lo), y: 4, z: 8, core: 2. Of those that a mesh axis runs over, the one named last changes fastest.
Arguments:
- pool: bfloat16 [327680, 4096], P(('cand', 'query')), may hold values from -6 to 6
- cand_ids: int32 [262144], P(('cand', 'query')), may hold values from 0 to 1279
- pick_ids: int32 [256], P(('cand', 'query')), may hold values from 0 to 1279
- queries: bfloat16 [1024, 4096], P('query'), may hold values from -6 to 6
Outputs:
- gains: float32 [262144], P(('cand', 'query'))
- coverage: float32 [1024], P('query')
Inputs may be any that keep to these rules, and one draw needn't show every extreme that they name: `cand_ids`: each id is a row within the pool block of 1280 rows that lies on the same device as the id. `pick_ids`: each id is a row within the pool block of 1280 rows that lies on the same device as the id.
All inputs are finite; a program needn't handle non-finite values.
Results may differ from a plain program's by a relative error of at most 0.0003.
Values may be sent and summed in bfloat16 or wider, within the bound.
A program may use at most 128 MiB of HBM per device.

v0:
```python
import math
import jax
import jax.numpy as jnp
from jax import lax
from jax.sharding import PartitionSpec as P

D = 4096


def similarity(rows, targets):
    product = lax.dot_general(
        rows, targets, (((1,), (1,)), ((), ())), preferred_element_type=jnp.float32
    )
    return product * (1.0 / math.sqrt(D))


def on_device(pool, cand_ids, pick_ids, queries):
    q_rows = queries.shape[0]
    candidates = jnp.take(pool, cand_ids, axis=0)
    picked = jnp.take(pool, pick_ids, axis=0)
    best = jnp.max(similarity(picked, lax.all_gather(queries, "query", axis=0, tiled=True)), axis=0)
    coverage = lax.pmax(best, ("cand", "query"))
    scores = similarity(candidates, lax.all_gather(queries, "query", axis=0, tiled=True))
    summed = jnp.sum(jnp.maximum(scores - coverage[None, :], 0.0), axis=1)
    highest = jnp.max(scores, axis=1)
    gained, highest = (summed, highest)
    gains = gained + 1.0 * highest
    own_cover = lax.dynamic_slice_in_dim(coverage, lax.axis_index("query") * q_rows, q_rows, 0)
    return (gains, own_cover)


def solution(mesh):
    in_specs = (
        P(("cand", "query"), None),
        P(("cand", "query")),
        P(("cand", "query")),
        P("query", None),
    )
    out_specs = (P(("cand", "query")), P("query"))
    return jax.shard_map(
        on_device, mesh=mesh, in_specs=in_specs, out_specs=out_specs, check_vma=False
    )
```

profile of v0, /device:TPU:1, one launch (start us, length us, event | category | flops | bytes accessed | tf_op | source)
XLA Modules:
  0.0 289.6 jit_solution(9840144230688379717)
XLA Ops:
  7.2 0.0 all-gather.2.cloned.1.call-start
  7.2 0.7 all-gather.2.cloned.1.call-update
  8.6 0.7 fusion.9
  9.2 0.0 copy-start
  9.3 20.4 %gather_fusion = bf16[1024,4096]{1,0:T(8,128)(2,1)} fusion(bf16[1280,4096]{1,0:T(8,128)(2,1)} %param.4, s32[1024]{0:T(1024)S(1)} %fusion.9), kind=kCustom, calls=%fused_computation | custom fusion | bytes 16781312 | tf_op jit(solution)/shard_map/jit(_take)/gather | solution.py:19
  29.7 0.0 copy-done
  29.7 154.8 %all-gather.2.cloned.1.call-done = bf16[1024,4096]{1,0:T(8,128)(2,1)} async-done(((bf16[128,4096]{1,0:T(8,128)(2,1)}), bf16[1024,4096]{1,0:T(8,128)(2,1)}) %all-gather.2.cloned.1.call-update) | async-done | bytes 8388624 | tf_op jit(solution)/shard_map/all_gather | solution.py:23
  184.5 5.7 %fusion.5 = f32[1,1024]{1,0:T(1,128)S(1)} fusion(bf16[1024,4096]{1,0:T(8,128)(2,1)} %all-gather.2.cloned.1.call-done, pred[]{:T(512)} %bitcast, bf16[1280,4096]{1,0:T(8,128)(2,1)} %param.4, s32[]{:T(128)} %bitcast.1), kind=kOutput, calls=%fused_computation.9 | convolution fusion | flops 8392704 | bytes 8410112 | tf_op jit(solution)/shard_map/dot_general | solution.py:11
  190.2 77.0 %pmax.7 = f32[1024]{0:T(1024)S(1)} all-reduce(f32[1024]{0:T(1024)S(1)} %broadcast_multiply_fusion), channel_id=1, replica_groups=mesh['cand'=32,'query'=8] {'cand','query'}, use_global_device_ids=true, to_apply=%region_0.1 | all-reduce | flops 1024 | bytes 8192 | tf_op jit(solution)/shard_map/pmax | solution.py:22
  267.2 0.6 dynamic_slice.3
  267.8 14.3 %multiply_reduce_fusion = (f32[1024]{0:T(1024)S(1)}, f32[1024]{0:T(1024)S(1)}) fusion(f32[1024]{0:T(1024)S(1)} %pmax.7, bf16[1024,4096]{1,0:T(8,128)(2,1)} %all-gather.2.cloned.1.call-done, bf16[1024,4096]{1,0:T(8,128)(2,1)} %gather_fusion, pred[1024]{0:T(1024)(128)(4,1)S(1)} %compare_and_fusion), kind=kOutput, calls=%fused_computation.6 | convolution fusion | flops 8599369728 | bytes 16790528 | tf_op jit(solution)/shard_map/dot_general | solution.py:11
  282.1 0.6 add.21
  (2 shorter events, 0.0 us)
Async XLA Ops:
  7.2 177.3 %all-gather.2.cloned.1.call-start = ((), (), s32[]{:S(2)}) async-start(), calls=%async_computation | async-start | bytes 9437184 | tf_op jit(solution)/shard_map/all_gather | solution.py:23
  9.2 20.4 %copy-start = (s32[1024]{0:T(1024)S(1)}, s32[1024]{0:T(1024)}, u32[]{:S(2)}) copy-start(s32[1024]{0:T(1024)} %param.5) | copy-start | bytes 12292
Sparse Core Ops, SparseCore 0:
  9.8 174.6 all-gather.1
where the time goes:
time: 290 us
  waiting for transfers between devices  155 us (53%)
  blocking collectives  77 us (27%)
  local copies, waits for them, and re-layouts  21 us (7%)
  matrix products  20 us (7%)
  between operations  14.7 us (5%)
    all_gather x1, waiting for transfers between devices, on_device(): lax.all_gather(queries, 'query', axis=0, tiled=True)  155 us
    pmax x1, blocking collectives, on_device(): coverage = lax.pmax(best, ('cand', 'query'))  77 us
    gather x1, local copies, waits for them, and re-layouts, on_device(): candidates = jnp.take(pool, cand_ids, axis=0)  20.4 us
    dot_general x2, matrix products, similarity(): lax.dot_general(rows, targets, (((1,), (1,)), ((), ())), preferred_elemen...  20 us
  transfers between devices with their start and end apart: 1, of which 1 were waited for; matrix products, arithmetic and copies ran while one was open for 7% of the time, Pallas kernels for 0%

commit v1 on v0

--- a/solution.py
+++ b/solution.py
@@ -20,7 +20,12 @@
     picked = jnp.take(pool, pick_ids, axis=0)
     best = jnp.max(similarity(picked, lax.all_gather(queries, "query", axis=0, tiled=True)), axis=0)
     coverage = lax.pmax(best, ("cand", "query"))
-    scores = similarity(candidates, lax.all_gather(queries, "query", axis=0, tiled=True))
+    scores = similarity(
+        candidates,
+        jnp.concatenate(
+            lax.all_to_all(jnp.stack([queries] * lax.axis_size("query")), "query", 0, 0), axis=0
+        ),
+    )
     summed = jnp.sum(jnp.maximum(scores - coverage[None, :], 0.0), axis=1)
     highest = jnp.max(scores, axis=1)
     gained, highest = (summed, highest)

time: 290 us -> 378 us (1.30)
  waiting for transfers between devices: 155 us -> 230 us
  starting transfers between devices: 0.04 us -> 6.12 us
  local copies, waits for them, and re-layouts: 21 us -> 26.5 us
    all_gather x1, waiting for transfers between devices: 155 us -> 229 us  [on_device(): lax.all_gather(queries, 'query', axis=0, tiled=True)]
    all_to_all x0 -> x1, starting transfers between devices: none -> 6.08 us  [on_device(): lax.all_to_all(jnp.stack([queries] * lax.axis_size('query')), 'query', 0, 0)]
    another operation x0 -> x1, local copies, waits for them, and re-layouts: none -> 5.49 us  [on_device(): jnp.stack([queries] * lax.axis_size('query'))]
  transfers between devices with their start and end apart: 1 -> 2, of which waited for: 1 -> 1; matrix products, arithmetic and copies ran while one was open for 7% -> 9% of each run, Pallas kernels for 0% -> 0%
where the time goes in v1:
time: 378 us; the launch traced here: 377 us
  waiting for transfers between devices  230 us (61%)
  blocking collectives  79.2 us (21%)
  local copies, waits for them, and re-layouts  26.5 us (7%)
  matrix products  20 us (5%)
  between operations  14.7 us (4%)
  starting transfers between devices  6.12 us (2%)
    all_gather x1, waiting for transfers between devices, on_device(): lax.all_gather(queries, 'query', axis=0, tiled=True)  229 us
    pmax x1, blocking collectives, on_device(): coverage = lax.pmax(best, ('cand', 'query'))  79.2 us
    gather x1, local copies, waits for them, and re-layouts, on_device(): candidates = jnp.take(pool, cand_ids, axis=0)  20.4 us
    dot_general x2, matrix products, similarity(): lax.dot_general(rows, targets, (((1,), (1,)), ((), ())), preferred_elemen...  20 us
  transfers between devices with their start and end apart: 2, of which 1 were waited for; matrix products, arithmetic and copies ran while one was open for 9% of the time, Pallas kernels for 0%

profile of v1, /device:TPU:1, one launch (start us, length us, event | category | flops | bytes accessed | tf_op | source)
XLA Modules:
  0.0 377.3 jit_solution(9991249686085127002)
XLA Ops:
  7.2 0.0 all-gather.2.cloned.1.call-start
  7.2 0.7 all-gather.2.cloned.1.call-update
  7.9 5.5 %stack.2 = bf16[8,128,4096]{2,1,0:T(8,128)(2,1)} broadcast(bf16[128,4096]{1,0:T(8,128)(2,1)} %param.7), dimensions={1,2} | broadcast | bytes 9437184 | tf_op jit(solution)/shard_map/stack | solution.py:26
  13.4 0.0 copy-start
  13.4 6.1 %all-to-all-start = ((bf16[8,128,4096]{2,1,0:T(8,128)(2,1)}), bf16[8,128,4096]{2,1,0:T(8,128)(2,1)}, u32[]{:S(2)}, u32[]{:S(2)}) async-start(bf16[8,128,4096]{2,1,0:T(8,128)(2,1)} %stack.2), calls=%async_computation | async-start | bytes 16777216 | tf_op jit(solution)/shard_map/all_to_all | solution.py:26
  20.1 0.0 copy-done
  20.2 20.4 %gather_fusion = bf16[1024,4096]{1,0:T(8,128)(2,1)} fusion(bf16[1280,4096]{1,0:T(8,128)(2,1)} %param.4, s32[1024]{0:T(1024)S(1)} %fusion.9), kind=kCustom, calls=%fused_computation | custom fusion | bytes 16781312 | tf_op jit(solution)/shard_map/jit(_take)/gather | solution.py:19
  40.6 229.5 %all-gather.2.cloned.1.call-done = bf16[1024,4096]{1,0:T(8,128)(2,1)} async-done(((bf16[128,4096]{1,0:T(8,128)(2,1)}), bf16[1024,4096]{1,0:T(8,128)(2,1)}) %all-gather.2.cloned.1.call-update) | async-done | bytes 8388624 | tf_op jit(solution)/shard_map/all_gather | solution.py:21
  270.1 5.7 %fusion.5 = f32[1,1024]{1,0:T(1,128)S(1)} fusion(bf16[1024,4096]{1,0:T(8,128)(2,1)} %all-gather.2.cloned.1.call-done, pred[]{:T(512)} %bitcast.1, bf16[1280,4096]{1,0:T(8,128)(2,1)} %param.4, s32[]{:T(128)} %bitcast.2), kind=kOutput, calls=%fused_computation.9 | convolution fusion | flops 8392704 | bytes 8410112 | tf_op jit(solution)/shard_map/dot_general | solution.py:11
  275.7 79.2 %pmax.7 = f32[1024]{0:T(1024)S(1)} all-reduce(f32[1024]{0:T(1024)S(1)} %broadcast_multiply_fusion), channel_id=1, replica_groups=mesh['cand'=32,'query'=8] {'cand','query'}, use_global_device_ids=true, to_apply=%region_0.1 | all-reduce | flops 1024 | bytes 8192 | tf_op jit(solution)/shard_map/pmax | solution.py:22
  354.9 0.6 dynamic_slice.3
  355.5 0.0 all-to-all-done
  355.5 14.3 %multiply_reduce_fusion = (f32[1024]{0:T(1024)S(1)}, f32[1024]{0:T(1024)S(1)}) fusion(f32[1024]{0:T(1024)S(1)} %pmax.7, bf16[1024,4096]{1,0:T(8,128)(2,1)} %bitcast, bf16[1024,4096]{1,0:T(8,128)(2,1)} %gather_fusion, pred[1024]{0:T(1024)(128)(4,1)S(1)} %compare_and_fusion), kind=kOutput, calls=%fused_computation.6 | convolution fusion | flops 8599369728 | bytes 16790528 | tf_op jit(solution)/shard_map/dot_general | solution.py:11
  369.9 0.6 add.21
  (3 shorter events, 0.0 us)
Async XLA Ops:
  7.2 262.9 %all-gather.2.cloned.1.call-start = ((), (), s32[]{:S(2)}) async-start(), calls=%async_computation.1 | async-start | bytes 9437184 | tf_op jit(solution)/shard_map/all_gather | solution.py:21
  13.4 6.7 %copy-start = (s32[1024]{0:T(1024)S(1)}, s32[1024]{0:T(1024)}, u32[]{:S(2)}) copy-start(s32[1024]{0:T(1024)} %param.5) | copy-start | bytes 12292
  13.4 342.1 %all-to-all-start = ((bf16[8,128,4096]{2,1,0:T(8,128)(2,1)}), bf16[8,128,4096]{2,1,0:T(8,128)(2,1)}, u32[]{:S(2)}, u32[]{:S(2)}) async-start(bf16[8,128,4096]{2,1,0:T(8,128)(2,1)} %stack.2), calls=%async_computation | async-start | bytes 16777216 | tf_op jit(solution)/shard_map/all_to_all | solution.py:26
Sparse Core Ops, SparseCore 0:
  9.8 260.2 all-gather.1
